TPU v7x, 32 devices: a whole 2x2x4 slice. The times are simulated.
32 devices in a mesh: seq: 8 (over y, x, core), head: 4 (over z).
Axes of the slice: x: 2, y: 2, z: 4, core: 2. Of those that a mesh axis runs over, the one named last changes fastest.
Arguments:
- tokens: bfloat16 [32, 512, 1024], P('seq', 'head'), may hold values from -6 to 6
- lengths: int32 [32], P('seq'), may hold values from 128 to 512, as said below
- separators: int32 [32], P('seq'), may hold values from 32 to 383, as said below
- type_table: float32 [2, 1024], replicated, may hold values from -3 to 3
- project_in: bfloat16 [2, 1024, 3072], P(None, 'seq'), may hold values from -0.1875 to 0.1875
- project_out: bfloat16 [2, 1024, 1024], P(None, 'seq'), may hold values from -0.75 to 0.75
- up_weight: bfloat16 [2, 1024, 4096], P(None, 'seq', 'head'), may hold values from -0.1875 to 0.1875
- down_weight: bfloat16 [2, 4096, 1024], P(None, 'head', 'seq'), may hold values from -0.09375 to 0.09375
- first_norm_gain: float32 [2, 1024], replicated, may hold values from 0.5 to 1.5
- second_norm_gain: float32 [2, 1024], replicated, may hold values from 0.5 to 1.5
- query_bias: float32 [2, 1024], replicated, may hold values from -3 to 3
- value_bias: float32 [2, 1024], replicated, may hold values from -3 to 3
- output_bias: float32 [2, 1024], replicated, may hold values from -3 to 3
- first_norm_bias: float32 [2, 1024], replicated, may hold values from -3 to 3
- hidden_bias: float32 [2, 4096], replicated, may hold values from -3 to 3
- down_bias: float32 [2, 1024], replicated, may hold values from -3 to 3
- second_norm_bias: float32 [2, 1024], replicated, may hold values from -3 to 3
- cotangent: bfloat16 [32, 512, 1024], P('seq', 'head'), may hold values from -6 to 6
Outputs:
- activations: bfloat16 [32, 512, 1024], P('seq', 'head')
- input_grad: float32 [32, 512, 1024], P('seq', 'head')
- query_bias_grad: float32 [2, 1024], replicated
- value_bias_grad: float32 [2, 1024], replicated
- output_bias_grad: float32 [2, 1024], replicated
- first_norm_bias_grad: float32 [2, 1024], replicated
- hidden_bias_grad: float32 [2, 4096], replicated
- down_bias_grad: float32 [2, 1024], replicated
- second_norm_bias_grad: float32 [2, 1024], replicated
Inputs may be any that keep to these rules, and one draw needn't show every extreme that they name: `lengths`: in the 4 rows of each index of seq (rows k * 4 to (k + 1) * 4 - 1), one row uses all 512 slots. `separators`: each row's separator lies between a quarter and three quarters of its length.
All inputs are finite; a program needn't handle non-finite values.
Results may differ from a plain program's by a relative error of at most 0.017.
Values may be sent and summed in bfloat16 or wider, within the bound.
A program may use at most 192 MiB of HBM per device.

v0:
```python
from functools import partial

import jax
import jax.numpy as jnp
from jax import lax
from jax.sharding import PartitionSpec as P

HEAD_DIM = 64
LAYERS = 2


EPS = 1e-06
MASKED = -1000000000.0


def layer_norm(total, gain, bias):
    mean = jnp.mean(total, -1, keepdims=True)
    centered = total - mean
    spread = jnp.mean(centered * centered, -1, keepdims=True)
    return centered * lax.rsqrt(spread + EPS) * gain + bias


def gelu_exact(value):
    return jax.nn.gelu(value, approximate=False)


def contract_last(left, right):
    return lax.dot_general(
        left, right, (((1,), (1,)), ((), ())), preferred_element_type=jnp.float32
    )


def split_heads(block):
    return block.reshape(block.shape[0], -1, HEAD_DIM)


def masked_scores(queries, keys, length):
    scores = jnp.einsum(
        "qhd,khd->hqk", queries, keys, preferred_element_type=jnp.float32
    ) * HEAD_DIM ** (-0.5)
    valid = jnp.arange(keys.shape[0]) < length
    return jnp.where(valid[None, None, :], scores, MASKED)


def attend_forward(packed):
    projected, length = packed
    slots = projected.shape[0]
    queries = split_heads(projected[:, 0])
    keys = split_heads(projected[:, 1])
    values = split_heads(projected[:, 2])
    scores = masked_scores(queries, keys, length)
    peak = jnp.max(scores, -1, keepdims=True)
    expo = jnp.exp(scores - peak)
    total = jnp.sum(expo, -1, keepdims=True)
    probs = (expo / total).astype(jnp.bfloat16)
    mixed = jnp.einsum("hqk,khd->qhd", probs, values, preferred_element_type=jnp.float32)
    return (mixed.astype(jnp.bfloat16).reshape(slots, -1), (peak + jnp.log(total))[:, :, 0])


def attend_backward(packed):
    projected, length, log_total, grad_mixed = packed
    slots = projected.shape[0]
    queries = split_heads(projected[:, 0])
    keys = split_heads(projected[:, 1])
    values = split_heads(projected[:, 2])
    scores = masked_scores(queries, keys, length)
    probs = jnp.exp(scores - log_total[:, :, None])
    grad_out = split_heads(grad_mixed)
    grad_probs = jnp.einsum("qhd,khd->hqk", grad_out, values, preferred_element_type=jnp.float32)
    inner = jnp.sum(grad_probs * probs, -1, keepdims=True)
    grad_scores = (probs * (grad_probs - inner)).astype(jnp.bfloat16)
    scale = HEAD_DIM ** (-0.5)
    grad_queries = (
        jnp.einsum("hqk,khd->qhd", grad_scores, keys, preferred_element_type=jnp.float32) * scale
    )
    grad_keys = (
        jnp.einsum("hqk,qhd->khd", grad_scores, queries, preferred_element_type=jnp.float32) * scale
    )
    grad_values = jnp.einsum(
        "hqk,qhd->khd", probs.astype(jnp.bfloat16), grad_out, preferred_element_type=jnp.float32
    )
    stacked = jnp.stack([grad_queries, grad_keys, grad_values], 1)
    return stacked.reshape(slots, 3, -1).astype(jnp.bfloat16)


def feed_forward(rows, up_part, down_part, bias_part):
    hidden = jnp.dot(rows, up_part, preferred_element_type=jnp.float32) + bias_part
    active = gelu_exact(hidden).astype(jnp.bfloat16)
    return jnp.dot(active, down_part, preferred_element_type=jnp.float32)


def local(
    tokens,
    lengths,
    separators,
    type_table,
    project_in,
    project_out,
    up_weight,
    down_weight,
    first_norm_gain,
    second_norm_gain,
    query_bias,
    value_bias,
    output_bias,
    first_norm_bias,
    hidden_bias,
    down_bias,
    second_norm_bias,
    cotangent,
):
    row_count, slot_part, width = tokens.shape
    token_count = row_count * slot_part
    hidden_part = up_weight.shape[2]
    offset = lax.axis_index("head") * hidden_part
    positions = lax.axis_index("head") * slot_part + jnp.arange(slot_part)
    second = (positions[None, :] > separators[:, None]) & (positions[None, :] < lengths[:, None])
    state = tokens.astype(jnp.float32) + jnp.where(second[:, :, None], type_table[1], type_table[0])
    state = state.reshape(token_count, width)

    def fetch(layer):
        gathered = (
            lax.all_gather(project_in[layer], "seq", axis=0, tiled=True),
            lax.all_gather(project_out[layer], "seq", axis=0, tiled=True),
            lax.all_gather(up_weight[layer], "seq", axis=0, tiled=True),
            lax.all_gather(down_weight[layer], "seq", axis=1, tiled=True),
        )
        return (gathered[0], gathered[1], gathered[2], gathered[3])

    def layer_hidden_bias(layer):
        return lax.dynamic_slice_in_dim(hidden_bias[layer], offset, hidden_part, 0)

    saved = []
    for layer in range(LAYERS):
        weights = fetch(layer)
        inner_in, inner_out, up_part, down_part = weights
        joined = jnp.concatenate(
            [query_bias[layer], jnp.zeros_like(query_bias[layer]), value_bias[layer]]
        )
        projected = (
            jnp.dot(state.astype(jnp.bfloat16), inner_in, preferred_element_type=jnp.float32)
            + joined
        ).astype(jnp.bfloat16)
        heads = lax.all_to_all(
            projected.reshape(row_count, slot_part, 3, width),
            "head",
            split_axis=3,
            concat_axis=1,
            tiled=True,
        )
        mixed, log_total = lax.map(attend_forward, (heads, lengths))
        mixed = lax.all_to_all(mixed, "head", split_axis=1, concat_axis=2, tiled=True).reshape(
            token_count, width
        )
        first_sum = (
            state
            + jnp.dot(mixed, inner_out, preferred_element_type=jnp.float32)
            + output_bias[layer]
        )
        normed = layer_norm(first_sum, first_norm_gain[layer], first_norm_bias[layer])
        normed_low = normed.astype(jnp.bfloat16)
        bias_part = layer_hidden_bias(layer)
        rows_all = lax.all_gather(normed_low[None], "head", axis=0, tiled=True).reshape(-1, width)
        branch_out = lax.psum_scatter(
            feed_forward(rows_all, up_part, down_part, bias_part).astype(jnp.bfloat16),
            "head",
            scatter_dimension=0,
            tiled=True,
        ).astype(jnp.float32)
        second_sum = normed + branch_out + down_bias[layer]
        saved.append((heads, log_total, first_sum, second_sum, rows_all))
        state = layer_norm(second_sum, second_norm_gain[layer], second_norm_bias[layer])
    activations = state.astype(jnp.bfloat16).reshape(row_count, slot_part, width)
    grad = cotangent.astype(jnp.float32).reshape(token_count, width)
    query_grads = [None] * LAYERS
    value_grads = [None] * LAYERS
    output_grads = [None] * LAYERS
    first_grads = [None] * LAYERS
    hidden_grads = [None] * LAYERS
    down_grads = [None] * LAYERS
    second_grads = [None] * LAYERS
    for layer in reversed(range(LAYERS)):
        heads, log_total, first_sum, second_sum, rows_all = saved[layer]
        weights = fetch(layer)
        inner_in, inner_out, up_part, down_part = weights
        second_grads[layer] = jnp.sum(grad, 0)
        _, norm_back = jax.vjp(
            partial(layer_norm, gain=second_norm_gain[layer], bias=second_norm_bias[layer]),
            second_sum,
        )
        grad_second = norm_back(grad)[0]
        down_grads[layer] = jnp.sum(grad_second, 0)
        grad_low = grad_second.astype(jnp.bfloat16)
        bias_part = layer_hidden_bias(layer)
        grad_rows = lax.all_gather(grad_low[None], "head", axis=0, tiled=True).reshape(-1, width)
        hidden = jnp.dot(rows_all, up_part, preferred_element_type=jnp.float32) + bias_part
        grad_active = contract_last(grad_rows, down_part)
        _, gelu_back = jax.vjp(gelu_exact, hidden)
        grad_hidden = gelu_back(grad_active)[0]
        hidden_local = jnp.sum(grad_hidden, 0)
        grad_hidden_low = grad_hidden.astype(jnp.bfloat16)
        hidden_grads[layer] = lax.dynamic_update_slice_in_dim(
            jnp.zeros_like(hidden_bias[layer]), hidden_local, offset, 0
        )
        grad_normed = grad_second + lax.psum_scatter(
            contract_last(grad_hidden_low, up_part).astype(jnp.bfloat16),
            "head",
            scatter_dimension=0,
            tiled=True,
        ).astype(jnp.float32)
        first_grads[layer] = jnp.sum(grad_normed, 0)
        _, norm_back = jax.vjp(
            partial(layer_norm, gain=first_norm_gain[layer], bias=first_norm_bias[layer]), first_sum
        )
        grad_first = norm_back(grad_normed)[0]
        output_grads[layer] = jnp.sum(grad_first, 0)
        grad_mixed = contract_last(grad_first.astype(jnp.bfloat16), inner_out).astype(jnp.bfloat16)
        grad_heads = lax.all_to_all(
            grad_mixed.reshape(row_count, slot_part, width),
            "head",
            split_axis=2,
            concat_axis=1,
            tiled=True,
        )
        grad_projected = lax.map(attend_backward, (heads, lengths, log_total, grad_heads))
        grad_projected = lax.all_to_all(
            grad_projected, "head", split_axis=1, concat_axis=3, tiled=True
        ).reshape(token_count, 3 * width)
        query_grads[layer] = jnp.sum(grad_projected[:, :width], 0, dtype=jnp.float32)
        value_grads[layer] = jnp.sum(grad_projected[:, 2 * width :], 0, dtype=jnp.float32)
        grad = grad_first + contract_last(grad_projected, inner_in)
    summed = lax.psum(
        (
            jnp.stack(query_grads),
            jnp.stack(value_grads),
            jnp.stack(output_grads),
            jnp.stack(first_grads),
            jnp.stack(hidden_grads),
            jnp.stack(down_grads),
            jnp.stack(second_grads),
        ),
        ("seq", "head"),
    )
    input_grad = grad.reshape(row_count, slot_part, width)
    return (
        activations,
        input_grad,
        summed[0],
        summed[1],
        summed[2],
        summed[3],
        summed[4],
        summed[5],
        summed[6],
    )


def solution(mesh):
    placed = (
        P("seq", "head", None),
        P("seq"),
        P("seq"),
        P(),
        P(None, "seq", None),
        P(None, "seq", None),
        P(None, "seq", "head"),
        P(None, "head", "seq"),
        P(),
        P(),
        P(),
        P(),
        P(),
        P(),
        P(),
        P(),
        P(),
        P("seq", "head", None),
    )
    return jax.shard_map(
        local,
        mesh=mesh,
        in_specs=placed,
        out_specs=(
            P("seq", "head", None),
            P("seq", "head", None),
            P(),
            P(),
            P(),
            P(),
            P(),
            P(),
            P(),
        ),
        check_vma=False,
    )
```

profile of v0, /device:TPU:0, one launch (start us, length us, event | category | flops | bytes accessed | tf_op | source)
XLA Modules:
  0.0 1686.5 jit_solution(3890517933213793113)
XLA Ops:
  7.2 2.7 fusion.146
  16.4 41.9 %all-gather.25.cloned.1.call-done = bf16[1,1024,3072]{2,1,0:T(8,128)(2,1)} async-done(((bf16[1,128,3072]{2,1,0:T(8,128)(2,1)}), bf16[1,1024,3072]{2,1,0:T(8,128)(2,1)}) %all-gather.25.cloned.1.call-update) | async-done | bytes 6291472 | tf_op jit(solution)/shard_map/all_gather | solution.py:123
  58.3 6.5 add_convert_fusion.1
  64.9 6.1 reshape.459
  71.0 7.4 copy.122
  78.3 4.6 all-to-all-start
  86.8 67.2 %all-to-all-done = bf16[4,128,3,1024]{1,0,2,3:T(4,128)(2,1)S(1)} async-done(((bf16[4,128,3,1024]{1,0,2,3:T(4,128)(2,1)}), bf16[4,128,3,1024]{1,0,2,3:T(4,128)(2,1)S(1)}, u32[]{:S(2)}, u32[]{:S(2)}) %all-to-all-start) | async-done | bytes 3145760 | tf_op jit(solution)/shard_map/all_to_all | solution.py:144
  156.2 4.6 copy.124
  160.9 3.2 copy.125
  165.1 21.2 %while.44 = (s32[]{:T(128)}, bf16[4,512,256]{1,2,0:T(8,128)(2,1)}, f32[4,4,512]{2,1,0:T(4,128)S(1)}, bf16[4,512,3,256]{1,3,2,0:T(8,128)(2,1)S(1)}, s32[4]{0:T(128)S(1)}, /*index=5*/s32[]{:T(128)}) while((s32[]{:T(128)}, bf16[4,512,256]{1,2,0:T(8,128)(2,1)}, f32[4,4,512]{2,1,0:T(4,128)S(1)}, bf16[4,512,3,256]{1,3,2,0:T(8,128)(2,1)S(1)}, ...), condition=%wide.region_3.4_spmd, body=%wide.region_0.3_spmd.sunk | while | flops 281147904 | bytes 17369692 | solution.py:151
  186.3 3.2 copy.126
  189.5 4.2 all-to-all-start.1
  195.8 23.3 %all-to-all-done.1 = bf16[4,512,256]{2,0,1:T(4,128)(2,1)} async-done(((bf16[4,512,256]{2,0,1:T(4,128)(2,1)}), bf16[4,512,256]{2,0,1:T(4,128)(2,1)}, u32[]{:S(2)}, u32[]{:S(2)}) %all-to-all-start.1) | async-done | bytes 1048608 | tf_op jit(solution)/shard_map/all_to_all | solution.py:152
  222.3 3.9 fusion.160
  229.7 77.4 %all-gather.29.cloned.1.call-done = bf16[2048,1024]{1,0:T(8,128)(2,1)} async-done(((bf16[512,1024]{1,0:T(8,128)(2,1)}), bf16[2048,1024]{1,0:T(8,128)(2,1)}) %all-gather.29.cloned.1.call-update) | async-done | bytes 4194320 | tf_op jit(solution)/shard_map/all_gather | solution.py:163
  307.1 25.3 %fusion.34 = (f32[2048,1024]{1,0:T(8,128)}, f32[2048,1024]{1,0:T(8,128)}) fusion(f32[1024]{0:T(1024)S(1)} %bitcast.453, bf16[2048,1024]{1,0:T(8,128)(2,1)} %all-gather.29.cloned.1.call-done, bf16[1,1024,1024]{2,1,0:T(8,128)(2,1)} %all-gather.31.cloned.1.call-done), kind=kOutput, calls=%fused_computation.64 | convolution fusion | flops 4427087872 | bytes 23072768 | tf_op jit(solution)/shard_map/dot_general | solution.py:87
  332.4 3.7 all-gather.33.cloned.1.call-done
  336.1 12.9 fusion.75
  351.6 74.3 %reduce-scatter.5.cloned.1.call-done = bf16[512,1024]{1,0:T(8,128)(2,1)} async-done(((bf16[2048,1024]{1,0:T(8,128)(2,1)}), bf16[512,1024]{1,0:T(8,128)(2,1)}) %reduce-scatter.5.cloned.1.call-update) | async-done | bytes 1048592 | tf_op jit(solution)/shard_map/reduce_scatter | solution.py:164
  430.2 43.8 %all-gather.35.cloned.1.call-done = bf16[1,1024,3072]{2,1,0:T(8,128)(2,1)} async-done(((bf16[1,128,3072]{2,1,0:T(8,128)(2,1)}), bf16[1,1024,3072]{2,1,0:T(8,128)(2,1)}) %all-gather.35.cloned.1.call-update) | async-done | bytes 6291472 | tf_op jit(solution)/shard_map/all_gather | solution.py:123
  474.1 7.0 add_convert_fusion
  481.0 6.1 reshape.460
  487.1 7.5 copy.129
  494.6 4.6 all-to-all-start.2
  500.7 69.6 %all-to-all-done.2 = bf16[4,128,3,1024]{1,0,2,3:T(4,128)(2,1)S(1)} async-done(((bf16[4,128,3,1024]{1,0,2,3:T(4,128)(2,1)}), bf16[4,128,3,1024]{1,0,2,3:T(4,128)(2,1)S(1)}, u32[]{:S(2)}, u32[]{:S(2)}) %all-to-all-start.2) | async-done | bytes 3145760 | tf_op jit(solution)/shard_map/all_to_all | solution.py:144
  570.3 2.2 copy.130
  572.5 4.6 copy.131
  577.1 3.2 copy.132
  581.4 21.2 %while.45 = (s32[]{:T(128)}, bf16[4,512,256]{1,2,0:T(8,128)(2,1)}, f32[4,4,512]{2,1,0:T(4,128)S(1)}, bf16[4,512,3,256]{1,3,2,0:T(8,128)(2,1)S(1)}, s32[4]{0:T(128)S(1)}, /*index=5*/s32[]{:T(128)}) while((s32[]{:T(128)}, bf16[4,512,256]{1,2,0:T(8,128)(2,1)}, f32[4,4,512]{2,1,0:T(4,128)S(1)}, bf16[4,512,3,256]{1,3,2,0:T(8,128)(2,1)S(1)}, ...), condition=%wide.region_12.13_spmd, body=%wide.region_9.12_spmd.sunk | while | flops 281147904 | bytes 17369692 | solution.py:151
  602.5 3.1 copy.133
  605.6 29.0 %all_to_all.132 = bf16[4,512,256]{2,0,1:T(4,128)(2,1)S(1)} all-to-all(bf16[4,512,256]{2,0,1:T(4,128)(2,1)} %copy.133), channel_id=1, replica_groups=mesh['seq'=8,'head'=4] {'head'}, dimensions={1} | all-to-all | bytes 2097152 | tf_op jit(solution)/shard_map/all_to_all | solution.py:152
  636.6 4.0 fusion.161
  643.9 77.6 %all-gather.39.cloned.1.call-done = bf16[2048,1024]{1,0:T(8,128)(2,1)} async-done(((bf16[512,1024]{1,0:T(8,128)(2,1)}), bf16[2048,1024]{1,0:T(8,128)(2,1)}) %all-gather.39.cloned.1.call-update) | async-done | bytes 4194320 | tf_op jit(solution)/shard_map/all_gather | solution.py:163
  721.5 25.4 %fusion.35 = (f32[2048,1024]{1,0:T(8,128)}, f32[2048,1024]{1,0:T(8,128)}) fusion(f32[1024]{0:T(1024)S(1)} %bitcast.458, bf16[2048,1024]{1,0:T(8,128)(2,1)} %all-gather.39.cloned.1.call-done, bf16[1,1024,1024]{2,1,0:T(8,128)(2,1)} %all-gather.41.cloned.1.call-done), kind=kOutput, calls=%fused_computation.65 | convolution fusion | flops 4427087872 | bytes 23072768 | tf_op jit(solution)/shard_map/dot_general | solution.py:87
  746.9 3.4 all-gather.43.cloned.1.call-done
  750.3 12.9 fusion.74
  763.5 76.7 %reduce-scatter.7.cloned.1.call-done = bf16[512,1024]{1,0:T(8,128)(2,1)} async-done(((bf16[2048,1024]{1,0:T(8,128)(2,1)}), bf16[512,1024]{1,0:T(8,128)(2,1)}) %reduce-scatter.7.cloned.1.call-update) | async-done | bytes 1048592 | tf_op jit(solution)/shard_map/reduce_scatter | solution.py:164
  847.3 81.4 %all-gather.45.cloned.1.call-done = bf16[2048,1024]{1,0:T(8,128)(2,1)} async-done(((bf16[512,1024]{1,0:T(8,128)(2,1)}), bf16[2048,1024]{1,0:T(8,128)(2,1)}) %all-gather.45.cloned.1.call-update) | async-done | bytes 4194320 | tf_op jit(solution)/shard_map/all_gather | solution.py:195
  928.7 14.0 fusion.162
  942.7 6.3 fusion.68
  949.0 75.4 %reduce-scatter.9.cloned.1.call-done = bf16[512,1024]{1,0:T(8,128)(2,1)} async-done(((bf16[2048,1024]{1,0:T(8,128)(2,1)}), bf16[512,1024]{1,0:T(8,128)(2,1)}) %reduce-scatter.9.cloned.1.call-update) | async-done | bytes 1048592 | tf_op jit(solution)/shard_map/reduce_scatter | solution.py:205
  1024.5 3.5 fusion.133
  1033.1 4.2 all-to-all-start.4
  1037.7 25.4 %all-to-all-done.4 = bf16[4,128,1024]{1,0,2:T(4,128)(2,1)S(1)} async-done(((bf16[4,128,1024]{1,0,2:T(4,128)(2,1)}), bf16[4,128,1024]{1,0,2:T(4,128)(2,1)S(1)}, u32[]{:S(2)}, u32[]{:S(2)}) %all-to-all-start.4) | async-done | bytes 1048608 | tf_op jit(solution)/shard_map/all_to_all | solution.py:218
  1065.4 38.3 %while.46 = (s32[]{:T(128)}, bf16[4,512,3,256]{1,3,2,0:T(8,128)(2,1)S(1)}, bf16[4,512,3,256]{1,3,2,0:T(8,128)(2,1)}, s32[4]{0:T(128)S(1)}, f32[4,4,512]{2,1,0:T(...) while((s32[]{:T(128)}, bf16[4,512,3,256]{1,3,2,0:T(8,128)(2,1)S(1)}, ...), condition=%wide.region_25.26_spmd, body=%wide.region_23.25_spmd.sunk | while | flops 689830400 | bytes 39381100 | solution.py:225
  1103.7 3.8 copy.138
  1107.5 74.0 %all_to_all.133 = bf16[4,512,3,256]{3,0,2,1:T(4,128)(2,1)S(1)} all-to-all(bf16[4,512,3,256]{3,0,2,1:T(4,128)(2,1)} %copy.138), channel_id=1, replica_groups=mesh['seq'=8,'head'=4] {'head'}, dimensions={1} | all-to-all | bytes 6291456 | tf_op jit(solution)/shard_map/all_to_all | solution.py:226
  1181.5 4.1 copy.162
  1185.6 6.6 reshape.438
  1192.2 8.1 fusion.135
  1203.8 79.7 %all-gather.47.cloned.1.call-done = bf16[2048,1024]{1,0:T(8,128)(2,1)} async-done(((bf16[512,1024]{1,0:T(8,128)(2,1)}), bf16[2048,1024]{1,0:T(8,128)(2,1)}) %all-gather.47.cloned.1.call-update) | async-done | bytes 4194320 | tf_op jit(solution)/shard_map/all_gather | solution.py:195
  1283.5 13.3 fusion.163
  1296.8 6.3 fusion.71
  1303.2 75.5 %reduce-scatter.11.cloned.1.call-done = bf16[512,1024]{1,0:T(8,128)(2,1)} async-done(((bf16[2048,1024]{1,0:T(8,128)(2,1)}), bf16[512,1024]{1,0:T(8,128)(2,1)}) %reduce-scatter.11.cloned.1.call-update) | async-done | bytes 1048592 | tf_op jit(solution)/shard_map/reduce_scatter | solution.py:205
  1378.7 2.9 fusion.134
  1386.0 30.0 %all_to_all.134 = bf16[4,128,1024]{1,0,2:T(4,128)(2,1)S(1)} all-to-all(bf16[4,128,1024]{1,0,2:T(4,128)(2,1)S(1)} %copy.140), channel_id=1, replica_groups=mesh['seq'=8,'head'=4] {'head'}, dimensions={2} | all-to-all | bytes 2097152 | tf_op jit(solution)/shard_map/all_to_all | solution.py:218
  1418.3 41.0 %while.47 = (s32[]{:T(128)}, bf16[4,512,3,256]{1,3,2,0:T(8,128)(2,1)S(1)}, bf16[4,512,3,256]{1,3,2,0:T(8,128)(2,1)}, s32[4]{0:T(128)S(1)}, f32[4,4,512]{2,1,0:T(4,128)}, /*index=5*/bf16[4,512,256]{1,2,0:T(8,128)(2,1)}, s32[]{:T(128)}) while((s32[]{:T(128)}, bf16[4,512,3,256]{1,3,2,0:T(8,128)(2,1)S(1)}, bf16[4,512,3,256]{1,3,2,0:T(8,128)(2,1)}, ...), condition=%wide.region_33.34_spmd, body=%wide.region_31.33_spmd.sunk | while | flops 689830400 | bytes 39381100 | solution.py:225
  1459.3 3.8 copy.143
  1463.1 3.8 all-to-all-start.7
  1473.5 63.3 %all-to-all-done.7 = bf16[4,512,3,256]{3,0,2,1:T(4,128)(2,1)S(1)} async-done(((bf16[4,512,3,256]{3,0,2,1:T(4,128)(2,1)}), bf16[4,512,3,256]{3,0,2,1:T(4,128)(2,1)S(1)}, u32[]{:S(2)}, u32[]{:S(2)}) %all-to-all-start.7) | async-done | bytes 3145760 | tf_op jit(solution)/shard_map/all_to_all | solution.py:226
  1536.8 4.1 copy.161
  1540.9 5.2 reshape.441
  1547.0 7.8 add_add_fusion.7
  1554.8 115.5 %all-reduce.3.cloned.1.call-done = (f32[2,1024]{1,0:T(2,128)}, f32[2,1024]{1,0:T(2,128)}, f32[2,1024]{1,0:T(2,128)}, f32[2,1024]{1,0:T(2,128)}, f32[2,4096]{1,0:...) async-done(((f32[2,1024]{1,0:T(2,128)}, f32[2,1024]{1,0:T(2,128)}, f32[2,1024]{1,0:T(2,128)}, f32[2,1024]{1,0:T(2,128)}, f32[2,4096]{1,0:T(2,128)}, ...) | async-done | bytes 81936 | tf_op jit(solution)/shard_map/psum | solution.py:232
  (425 shorter events, 199.4 us)
Async XLA Ops:
  7.2 6.5 copy-start.18
  7.2 51.2 %all-gather.25.cloned.1.call-start = ((), (), s32[]{:S(2)}) async-start(), calls=%async_computation.16 | async-start | bytes 7077888 | tf_op jit(solution)/shard_map/all_gather | solution.py:123
  78.3 75.7 %all-to-all-start = ((bf16[4,128,3,1024]{1,0,2,3:T(4,128)(2,1)}), bf16[4,128,3,1024]{1,0,2,3:T(4,128)(2,1)S(1)}, u32[]{:S(2)}, u32[]{:S(2)}) async-start(bf16[4,128,3,1024]{1,0,2,3:T(4,128)(2,1)} %copy.122), calls=%async_computation | async-start | bytes 6291456 | tf_op jit(solution)/shard_map/all_to_all | solution.py:144
  82.9 139.4 %all-gather.27.cloned.1.call-start = ((), (), s32[]{:S(2)}) async-start(), calls=%async_computation.17 | async-start | bytes 2359296 | tf_op jit(solution)/shard_map/all_gather | solution.py:124
  84.8 144.8 %all-gather.31.cloned.1.call-start = ((), (), s32[]{:S(2)}) async-start(), calls=%async_computation.19 | async-start | bytes 2359296 | tf_op jit(solution)/shard_map/all_gather | solution.py:125
  160.9 4.3 copy-start.56
  186.3 36.0 %copy-start.2 = (bf16[4,512,3,256]{1,3,2,0:T(8,128)(2,1)}, bf16[4,512,3,256]{1,3,2,0:T(8,128)(2,1)S(1)}, u32[]{:S(2)}) copy-start(bf16[4,512,3,256]{1,3,2,0:T(8,128)(2,1)S(1)} %get-tuple-element.647) | copy-start | bytes 9437188
  186.3 36.0 %copy-start.20 = (f32[4,4,512]{2,1,0:T(4,128)}, f32[4,4,512]{2,1,0:T(4,128)S(1)}, u32[]{:S(2)}) copy-start(f32[4,4,512]{2,1,0:T(4,128)S(1)} %get-tuple-element.591) | copy-start | bytes 98308
  186.3 7.7 copy-start.46
  186.3 8.3 copy-start.47
  186.3 8.9 copy-start.48
  189.5 29.6 %all-to-all-start.1 = ((bf16[4,512,256]{2,0,1:T(4,128)(2,1)}), bf16[4,512,256]{2,0,1:T(4,128)(2,1)}, u32[]{:S(2)}, u32[]{:S(2)}) async-start(bf16[4,512,256]{2,0,1:T(4,128)(2,1)} %copy.126), calls=%async_computation.1 | async-start | bytes 2097152 | tf_op jit(solution)/shard_map/all_to_all | solution.py:152
  193.7 113.4 %all-gather.29.cloned.1.call-start = ((), (), s32[]{:S(2)}) async-start(), calls=%async_computation.18 | async-start | bytes 5242880 | tf_op jit(solution)/shard_map/all_gather | solution.py:163
  195.2 230.8 %copy-start.21 = (f32[1,1024]{1,0:T(1,128)}, f32[1,1024]{1,0:T(1,128)S(1)}, u32[]{:S(2)}) copy-start(f32[1,1024]{1,0:T(1,128)S(1)} %get-tuple-element.314) | copy-start | bytes 12292
  226.2 199.7 %copy-start = (f32[512,1024]{1,0:T(8,128)}, f32[512,1024]{1,0:T(8,128)S(1)}, u32[]{:S(2)}) copy-start(f32[512,1024]{1,0:T(8,128)S(1)} %get-tuple-element.332) | copy-start | bytes 6291460
  226.3 199.7 %copy-start.24 = (f32[512]{0:T(512)}, f32[512]{0:T(512)S(1)}, u32[]{:S(2)}) copy-start(f32[512]{0:T(512)S(1)} %broadcast_multiply_fusion.3) | copy-start | bytes 6148
  226.6 199.3 %copy-start.28 = (f32[512]{0:T(512)}, f32[512]{0:T(512)S(1)}, u32[]{:S(2)}) copy-start(f32[512]{0:T(512)S(1)} %fusion.127) | copy-start | bytes 6148
  228.0 108.1 %all-gather.33.cloned.1.call-start = ((), (), s32[]{:S(2)}) async-start(), calls=%async_computation.20 | async-start | bytes 2359296 | tf_op jit(solution)/shard_map/all_gather | solution.py:126
  228.9 197.0 %reduce-scatter.5.cloned.1.call-start = ((), (), s32[]{:S(2)}) async-start(), calls=%async_computation.12 | async-start | bytes 5242880 | tf_op jit(solution)/shard_map/reduce_scatter | solution.py:164
  229.6 106.5 %copy-start.52 = (f32[1,1024]{1,0:T(1,128)}, f32[1,1024]{1,0:T(1,128)S(1)}, u32[]{:S(2)}) copy-start(f32[1,1024]{1,0:T(1,128)S(1)} %constant_dynamic-slice_fusion.3) | copy-start | bytes 12292
  349.0 125.0 %copy-start.43 = (f32[3072]{0:T(1024)S(1)}, f32[3072]{0:T(1024)}, u32[]{:S(2)}) copy-start(f32[3072]{0:T(1024)} %get-tuple-element.327) | copy-start | bytes 36868
  349.0 125.0 %all-gather.35.cloned.1.call-start = ((), (), s32[]{:S(2)}) async-start(), calls=%async_computation.21 | async-start | bytes 7077888 | tf_op jit(solution)/shard_map/all_gather | solution.py:123
  351.0 285.6 %copy-start.41 = (f32[1,1024]{1,0:T(1,128)}, f32[1,1024]{1,0:T(1,128)S(1)}, u32[]{:S(2)}) copy-start(f32[1,1024]{1,0:T(1,128)S(1)} %get-tuple-element.310) | copy-start | bytes 12292
  428.0 208.6 %copy-start.31 = (f32[512]{0:T(512)}, f32[512]{0:T(512)S(1)}, u32[]{:S(2)}) copy-start(f32[512]{0:T(512)S(1)} %broadcast_multiply_fusion.2) | copy-start | bytes 6148
  430.2 206.4 %copy-start.44 = (f32[512]{0:T(512)}, f32[512]{0:T(512)S(1)}, u32[]{:S(2)}) copy-start(f32[512]{0:T(512)S(1)} %fusion.128) | copy-start | bytes 6148
  494.6 75.7 %all-to-all-start.2 = ((bf16[4,128,3,1024]{1,0,2,3:T(4,128)(2,1)}), bf16[4,128,3,1024]{1,0,2,3:T(4,128)(2,1)S(1)}, u32[]{:S(2)}, u32[]{:S(2)}) async-start(bf16[4,128,3,1024]{1,0,2,3:T(4,128)(2,1)} %copy.129), calls=%async_computation.3 | async-start | bytes 6291456 | tf_op jit(solution)/shard_map/all_to_all | solution.py:144
  499.2 137.4 %all-gather.37.cloned.1.call-start = ((), (), s32[]{:S(2)}) async-start(), calls=%async_computation.22 | async-start | bytes 2359296 | tf_op jit(solution)/shard_map/all_gather | solution.py:124
  499.9 144.0 %all-gather.41.cloned.1.call-start = ((), (), s32[]{:S(2)}) async-start(), calls=%async_computation.24 | async-start | bytes 2359296 | tf_op jit(solution)/shard_map/all_gather | solution.py:125
  500.6 220.9 %all-gather.39.cloned.1.call-start = ((), (), s32[]{:S(2)}) async-start(), calls=%async_computation.23 | async-start | bytes 5242880 | tf_op jit(solution)/shard_map/all_gather | solution.py:163
  602.5 34.0 %copy-start.3 = (bf16[4,512,3,256]{1,3,2,0:T(8,128)(2,1)}, bf16[4,512,3,256]{1,3,2,0:T(8,128)(2,1)S(1)}, u32[]{:S(2)}) copy-start(bf16[4,512,3,256]{1,3,2,0:T(8,128)(2,1)S(1)} %get-tuple-element.648) | copy-start | bytes 9437188
  602.5 34.1 %copy-start.55 = (f32[1,1024]{1,0:T(1,128)S(1)}, f32[1,1024]{1,0:T(1,128)}, u32[]{:S(2)}) copy-start(f32[1,1024]{1,0:T(1,128)} %get-tuple-element.317) | copy-start | bytes 12292
  636.6 4.4 copy-start.23
  636.6 4.4 copy-start.26
  642.5 107.8 %all-gather.43.cloned.1.call-start = ((), (), s32[]{:S(2)}) async-start(), calls=%async_computation.25 | async-start | bytes 2359296 | tf_op jit(solution)/shard_map/all_gather | solution.py:126
  643.2 196.9 %reduce-scatter.7.cloned.1.call-start = ((), (), s32[]{:S(2)}) async-start(), calls=%async_computation.13 | async-start | bytes 5242880 | tf_op jit(solution)/shard_map/reduce_scatter | solution.py:164
  763.2 76.9 %copy-start.38 = (f32[1,1024]{1,0:T(1,128)S(1)}, f32[1,1024]{1,0:T(1,128)}, u32[]{:S(2)}) copy-start(f32[1,1024]{1,0:T(1,128)} %get-tuple-element.326) | copy-start | bytes 12292
  763.2 79.0 %copy-start.10 = (bf16[4,128,1024]{2,1,0:T(8,128)(2,1)S(1)}, bf16[4,128,1024]{2,1,0:T(8,128)(2,1)}, u32[]{:S(2)}) copy-start(bf16[4,128,1024]{2,1,0:T(8,128)(2,1)} %param.43) | copy-start | bytes 3145732
  763.2 79.0 %copy-start.27 = (f32[1,1024]{1,0:T(1,128)S(1)}, f32[1,1024]{1,0:T(1,128)}, u32[]{:S(2)}) copy-start(f32[1,1024]{1,0:T(1,128)} %get-tuple-element.309) | copy-start | bytes 12292
  763.2 165.5 %all-gather.45.cloned.1.call-start = ((), (), s32[]{:S(2)}) async-start(), calls=%async_computation.26 | async-start | bytes 5242880 | tf_op jit(solution)/shard_map/all_gather | solution.py:195
  847.2 177.2 %reduce-scatter.9.cloned.1.call-start = ((), (), s32[]{:S(2)}) async-start(), calls=%async_computation.14 | async-start | bytes 5242880 | tf_op jit(solution)/shard_map/reduce_scatter | solution.py:205
  928.7 14.0 copy-start.60
  1024.5 3.5 copy-start.16
  1033.1 30.0 %all-to-all-start.4 = ((bf16[4,128,1024]{1,0,2:T(4,128)(2,1)}), bf16[4,128,1024]{1,0,2:T(4,128)(2,1)S(1)}, u32[]{:S(2)}, u32[]{:S(2)}) async-start(bf16[4,128,1024]{1,0,2:T(4,128)(2,1)} %copy.135), calls=%async_computation.7 | async-start | bytes 2097152 | tf_op jit(solution)/shard_map/all_to_all | solution.py:218
  1037.3 246.2 %all-gather.47.cloned.1.call-start = ((), (), s32[]{:S(2)}) async-start(), calls=%async_computation.27 | async-start | bytes 5242880 | tf_op jit(solution)/shard_map/all_gather | solution.py:195
  1185.6 6.6 copy-start.9
  1185.6 6.6 copy-start.32
  1185.6 6.6 copy-start.42
  1192.2 8.1 copy-start.36
  1192.2 8.1 copy-start.45
  1200.4 83.1 %copy-start.53 = (f32[1,1024]{1,0:T(1,128)S(1)}, f32[1,1024]{1,0:T(1,128)}, u32[]{:S(2)}) copy-start(f32[1,1024]{1,0:T(1,128)} %copy-done.52) | copy-start | bytes 12292
  1203.6 93.2 %copy-start.58 = (bf16[1,1024,1024]{2,1,0:T(8,128)(2,1)S(1)}, bf16[1,1024,1024]{2,1,0:T(8,128)(2,1)}, u32[]{:S(2)}) copy-start(bf16[1,1024,1024]{2,1,0:T(8,128)(2,1)} %all-gather.31.cloned.1.call-done) | copy-start | bytes 6291460
  1203.6 175.1 %reduce-scatter.11.cloned.1.call-start = ((), (), s32[]{:S(2)}) async-start(), calls=%async_computation.15 | async-start | bytes 5242880 | tf_op jit(solution)/shard_map/reduce_scatter | solution.py:205
  1303.2 75.5 %copy-start.1 = (f32[512,1024]{1,0:T(8,128)S(1)}, f32[512,1024]{1,0:T(8,128)}, u32[]{:S(2)}) copy-start(f32[512,1024]{1,0:T(8,128)} %copy-done) | copy-start | bytes 6291460
  1303.2 75.5 %copy-start.22 = (f32[1,1024]{1,0:T(1,128)S(1)}, f32[1,1024]{1,0:T(1,128)}, u32[]{:S(2)}) copy-start(f32[1,1024]{1,0:T(1,128)} %copy-done.21) | copy-start | bytes 12292
  1303.2 75.5 %copy-start.25 = (f32[512]{0:T(512)S(1)}, f32[512]{0:T(512)}, u32[]{:S(2)}) copy-start(f32[512]{0:T(512)} %copy-done.24) | copy-start | bytes 6148
  1303.2 78.4 %copy-start.34 = (f32[512]{0:T(512)S(1)}, f32[512]{0:T(512)}, u32[]{:S(2)}) copy-start(f32[512]{0:T(512)} %copy-done.33) | copy-start | bytes 6148
  1303.2 78.5 %copy-start.29 = (f32[512]{0:T(512)S(1)}, f32[512]{0:T(512)}, u32[]{:S(2)}) copy-start(f32[512]{0:T(512)} %copy-done.28) | copy-start | bytes 6148
  1463.1 5.8 copy-start.54
  1463.1 73.7 %all-to-all-start.7 = ((bf16[4,512,3,256]{3,0,2,1:T(4,128)(2,1)}), bf16[4,512,3,256]{3,0,2,1:T(4,128)(2,1)S(1)}, u32[]{:S(2)}, u32[]{:S(2)}) async-start(bf16[4,512,3,256]{3,0,2,1:T(4,128)(2,1)} %copy.143), calls=%async_computation.11 | async-start | bytes 6291456 | tf_op jit(solution)/shard_map/all_to_all | solution.py:226
  1467.0 5.1 copy-start.40
  1467.0 5.9 copy-start.39
  1467.0 203.4 %all-reduce.3.cloned.1.call-start = ((), (), s32[]{:S(2)}) async-start(), calls=%async_computation.28 | async-start | bytes 163840 | tf_op jit(solution)/shard_map/psum | solution.py:232
  1467.3 3.7 copy-start.11
  1467.3 5.3 copy-start.14
  (19 other events, 36.6 us)
Sparse Core Ops, SparseCore 0:
  10.1 48.2 all-gather.24
  85.7 28.3 all-gather.26
  116.0 27.8 all-gather.30
  228.2 78.8 all-gather.28
  309.4 26.7 all-gather.32
  349.2 76.7 reduce-scatter.4
  428.0 46.0 all-gather.34
  502.0 28.3 all-gather.36
  532.5 27.8 all-gather.40
  642.6 78.8 all-gather.38
  723.5 26.7 all-gather.42
  763.3 76.7 reduce-scatter.6
  847.4 81.2 all-gather.44
  949.2 75.2 reduce-scatter.8
  1203.7 79.7 all-gather.46
  1303.3 75.2 reduce-scatter.10
  1547.2 123.1 all-reduce.2
where the time goes:
time: 1700 us; the launch traced here: 1690 us
  waiting for transfers between devices  1080 us (64%)
  matrix products  211 us (12%)
  local copies, waits for them, and re-layouts  164 us (10%)
  blocking collectives  133 us (8%)
  other arithmetic  60.7 us (4%)
  starting transfers between devices  23.8 us (1%)
    all_gather x2, waiting for transfers between devices, local(): lax.all_gather(grad_low[None], 'head', axis=0, tiled=True)  161 us
    all_gather x2, waiting for transfers between devices, local(): lax.all_gather(normed_low[None], 'head', axis=0, tiled=True)  155 us
    reduce_scatter x2, waiting for transfers between devices, local(): lax.psum_scatter(feed_forward(rows_all, up_part, down_part, bias_part).as...  151 us
    reduce_scatter x2, waiting for transfers between devices, local(): lax.psum_scatter(contract_last(grad_hidden_low, up_part).astype(jnp.bfloa...  151 us
    all_to_all x2, waiting for transfers between devices, local(): lax.all_to_all(projected.reshape(row_count, slot_part, 3, width), 'head',...  137 us
    psum x1, waiting for transfers between devices, local(): lax.psum((jnp.stack(query_grads), jnp.stack(value_grads), jnp.stack(outpu...  116 us
    all_gather x2, waiting for transfers between devices, fetch(): lax.all_gather(project_in[layer], 'seq', axis=0, tiled=True)  85.8 us
    all_to_all x1, blocking collectives, local(): lax.all_to_all(grad_projected, 'head', split_axis=1, concat_axis=3, tiled...  74 us
  transfers between devices with their start and end apart: 22, of which 18 were waited for; matrix products, arithmetic and copies ran while one was open for 10% of the time, Pallas kernels for 0%

commit v1 on v0

--- a/solution.py
+++ b/solution.py
@@ -1,16 +1,922 @@
-from functools import partial
+import functools
 
 import jax
 import jax.numpy as jnp
 from jax import lax
+from jax.experimental import pallas as pl
+from jax.experimental.pallas import tpu as pltpu
 from jax.sharding import PartitionSpec as P
 
+F32 = jnp.float32
+BF16 = jnp.bfloat16
+MESH = pl.DeviceIdType.MESH
 HEAD_DIM = 64
 LAYERS = 2
-
-
 EPS = 1e-06
 MASKED = -1000000000.0
+ROOT_HALF = 0.7071067811865476
+ROOT_TAU = 0.3989422804014327
+RING = 4
+WIDTH = 1024
+SLOTS = 512
+QUARTER = SLOTS // RING
+CHUNK = 256
+
+
+def nn(left, right):
+    return jnp.dot(left, right, preferred_element_type=F32)
+
+
+def nt(left, right):
+    return lax.dot_general(left, right, (((1,), (1,)), ((), ())), preferred_element_type=F32)
+
+
+def tn(left, right):
+    return lax.dot_general(left, right, (((0,), (0,)), ((), ())), preferred_element_type=F32)
+
+
+def place():
+    s, z = lax.axis_index("seq"), lax.axis_index("head")
+    c, x, y = lax.rem(s, 2), lax.rem(lax.div(s, 2), 2), lax.div(s, 4)
+    return s, z, c, x, y
+
+
+def peers(s, z, c, x, y):
+    return (s + 2 - 4 * x, z), (s + 4 - 8 * y, z), (s + 1 - 2 * c, z)
+
+
+def greet(near_x, near_y, twin, s, z):
+    barrier = pltpu.get_barrier_semaphore()
+    for device in (near_x, near_y, twin):
+        pl.semaphore_signal(barrier, inc=1, device_id=device, device_id_type=MESH)
+    for step in range(1, RING):
+        pl.semaphore_signal(
+            barrier, inc=1, device_id=(s, lax.rem(z + step, RING)), device_id_type=MESH
+        )
+    pl.semaphore_wait(barrier, 3 + RING - 1)
+
+
+def forward_kernel(
+    lengths_ref, separators_ref,
+    tokens_ref, cot_ref, in_ref, out_ref, up_ref,
+    down_ref, table_ref, gain1_ref, gain2_ref, qb_ref, vb_ref, ob_ref, b1_ref, hb_ref, db_ref, b2_ref,
+    g_in, g_out, g_ff, cot_row, act_row, s_qkv, s_mix, s_expo, s_inv, s_n, s_rs, s_gp,
+    tok_v, state_v, xb_v, qkv_v, mix_v, mixed_v, n_v, rs_v, normed_v, acc_v, active_v, gp_v, e_v, inv_v, w_v, dn_v,
+    tok_s, tok_r, cot_s, cot_r, at_s, at_r, ff_s, ff_r, z_s, z_r, f_s, f_r, cc_s, cc_r,
+    own_sem, dn_sem, w_sem, save_sem, e_sem, gp_sem,
+):
+    s, z, c, x, y = place()
+    near_x, near_y, twin = peers(s, z, c, x, y)
+    half = QUARTER // 2
+    A, B = pl.ds(0, half), pl.ds(half, half)
+    every = slice(None)
+    sent = []
+
+    def remote(src, dst, ss, rs, device):
+        return pltpu.make_async_remote_copy(
+            src_ref=src, dst_ref=dst, send_sem=ss, recv_sem=rs, device_id=device, device_id_type=MESH
+        )
+
+    def go(copy):
+        copy.start()
+        sent.append(copy)
+
+    own = []
+    for l in range(LAYERS):
+        own.append((
+            pltpu.make_async_copy(in_ref.at[l], g_in.at[l, y, x, c], own_sem.at[l, 0]),
+            pltpu.make_async_copy(out_ref.at[l], g_out.at[l, y, x, c], own_sem.at[l, 1]),
+            pltpu.make_async_copy(up_ref.at[l], g_ff.at[l, z, 0, y, x, c], own_sem.at[l, 2]),
+        ))
+    own_down = [
+        pltpu.make_async_copy(dn_v.at[l], g_ff.at[l, z, 1, y, x, c], dn_sem.at[l]) for l in range(LAYERS)
+    ]
+
+    gathered = (g_in, g_out)
+    shard = (in_ref, out_ref)
+
+    def at_first(l, t):
+        g = gathered[t]
+        return (
+            remote(shard[t].at[l, A], g.at[l, y, x, c, A], at_s.at[l, t, 0], at_r.at[l, t, 0], near_x),
+            remote(shard[t].at[l, B], g.at[l, y, x, c, B], at_s.at[l, t, 1], at_r.at[l, t, 1], near_y),
+        )
+
+    def at_last(l, t):
+        g = gathered[t]
+        pair, pile = g.at[l, y, every, c, A], g.at[l, every, x, c, B]
+        return (
+            remote(pair, pair, at_s.at[l, t, 2], at_r.at[l, t, 2], near_y),
+            remote(pile, pile, at_s.at[l, t, 3], at_r.at[l, t, 3], near_x),
+        )
+
+    def at_core(l, t):
+        part = gathered[t].at[l, every, every, c]
+        return remote(part, part, at_s.at[l, t, 4], at_r.at[l, t, 4], twin)
+
+    def at_send(l, t):
+        for copy in at_first(l, t):
+            go(copy)
+
+    def at_pass(l, t, side):
+        at_first(l, t)[side].wait_recv()
+        go(at_last(l, t)[side])
+
+    def at_share(l, t):
+        for copy in at_last(l, t):
+            copy.wait_recv()
+        go(at_core(l, t))
+
+    def rank(i):
+        near = z if i == 0 else None
+        if i == 0:
+            return near
+        low = jnp.where(z < 2, z, RING - 1 - z)
+        block = (1 - low) if i == 1 else i
+        return jnp.where(z < 2, block, RING - 1 - block)
+
+    def ff_part(l, block, side):
+        return g_ff.at[l, block, every, y, every, c, A] if side == 0 else g_ff.at[l, block, every, every, x, c, B]
+
+    def ff_first(l):
+        a, b = g_ff.at[l, z, every, y, x, c, A], g_ff.at[l, z, every, y, x, c, B]
+        return (
+            remote(a, a, ff_s.at[l, 0], ff_r.at[l, 0], near_x),
+            remote(b, b, ff_s.at[l, 1], ff_r.at[l, 1], near_y),
+        )
+
+    def ff_z(l, block, side, way):
+        part = ff_part(l, block, side)
+        beside = lax.rem(z + 1, RING) if way == 0 else lax.rem(z + RING - 1, RING)
+        return remote(part, part, z_s.at[l, block, side, way], z_r.at[l, block, side], (s, beside))
+
+    def ff_last(l, block, side):
+        part = ff_part(l, block, side)
+        return remote(part, part, f_s.at[l, block, side], f_r.at[l, block, side], near_y if side == 0 else near_x)
+
+    def ff_core(l, block):
+        part = g_ff.at[l, block, every, every, every, c]
+        return remote(part, part, cc_s.at[l, block], cc_r.at[l, block], twin)
+
+    right = z < RING - 1
+    left = z > 0
+
+    def ff_send(l):
+        for copy in ff_first(l):
+            go(copy)
+
+    def ff_spread(l, side):
+        ff_first(l)[side].wait_recv()
+        pl.when(right)(ff_z(l, z, side, 0).start)
+        pl.when(left)(ff_z(l, z, side, 1).start)
+
+    def ff_cross(l, i, side):
+        go(ff_last(l, rank(i), side))
+
+    def ff_relay(l, i, side):
+        block = rank(i)
+        ff_z(l, block, side, 0).wait_recv()
+        pl.when(jnp.logical_and(block < z, right))(ff_z(l, block, side, 0).start)
+        pl.when(jnp.logical_and(block > z, left))(ff_z(l, block, side, 1).start)
+
+    def ff_share(l, i):
+        block = rank(i)
+        for side in range(2):
+            ff_last(l, block, side).wait_recv()
+        go(ff_core(l, block))
+
+    def ff_drain(l):
+        for side in range(2):
+            for block in range(RING):
+                goes_right = jnp.logical_and(block <= z, right)
+                goes_left = jnp.logical_and(block >= z, left)
+                pl.when(goes_right)(ff_z(l, block, side, 0).wait_send)
+                pl.when(goes_left)(ff_z(l, block, side, 1).wait_send)
+
+    def row_copies(src, dst, ss, rs):
+        here = dst.at[pl.ds(pl.multiple_of(z * QUARTER, QUARTER), QUARTER)]
+        copies = []
+        for step in range(1, RING):
+            to = lax.rem(z + step, RING)
+            copies.append(remote(src.at[to], here, ss.at[step], rs.at[step], (s, to)))
+        return copies, pltpu.make_async_copy(src.at[z], here, ss.at[0])
+
+    def load(slot, src, width=WIDTH):
+        copy = pltpu.make_async_copy(src, w_v.at[slot], w_sem.at[slot])
+        copy.start()
+        return copy
+
+    def weight(slot, cols):
+        return w_v[slot, :, :, :, :, cols].reshape(WIDTH, CHUNK)
+
+    def weight_rows(slot, half_index):
+        return w_v[slot, half_index].reshape(SLOTS, WIDTH)
+
+    saves = {}
+    waiting = []
+
+    def save(key, src, dst, sem):
+        copy = pltpu.make_async_copy(src, dst, sem)
+        copy.start()
+        saves[key] = copy
+
+    def settle(key):
+        if key in saves:
+            saves.pop(key).wait()
+
+    def rows_loop(body, rows=64):
+        def step(r, carry):
+            body(pl.ds(pl.multiple_of(r * rows, rows), rows), r * rows)
+            return carry
+        lax.fori_loop(0, SLOTS // rows, step, 0)
+
+    def norm_rows(total, gain, bias, rr, which):
+        mean = jnp.sum(total, -1, keepdims=True) * (1.0 / WIDTH)
+        centered = total - mean
+        rs = lax.rsqrt(jnp.sum(centered * centered, -1, keepdims=True) * (1.0 / WIDTH) + EPS)
+        n = centered * rs
+        n_v[which, rr] = n.astype(BF16)
+        rs_v[which, rr] = rs + jnp.zeros((64, 128), F32)
+        return n * gain + bias
+
+    def start_state():
+        length, split = lengths_ref[z], separators_ref[z]
+
+        def body(rr, base):
+            pos = lax.broadcasted_iota(jnp.int32, (64, 1), 0) + base
+            second = jnp.logical_and(pos > split, pos < length)
+            kind = jnp.where(second, table_ref[1:2], table_ref[0:1])
+            value = tok_v[rr].astype(F32) + kind
+            state_v[rr] = value
+            xb_v[rr] = value.astype(BF16)
+        rows_loop(body)
+
+    def project(l):
+        settle("qkv")
+        loads = [load(j, g_in.at[l, :, :, :, :, pl.ds(j * WIDTH, WIDTH)]) for j in range(3)]
+        for j in range(3):
+            loads[j].wait()
+            for k in range(WIDTH // CHUNK):
+                cols = pl.ds(k * CHUNK, CHUNK)
+                value = nn(xb_v[...], weight(j, cols))
+                if j == 0:
+                    value = (value + qb_ref[l:l + 1, k * CHUNK:(k + 1) * CHUNK]).astype(BF16) * BF16(HEAD_DIM ** -0.5)
+                elif j == 2:
+                    value = value + vb_ref[l:l + 1, k * CHUNK:(k + 1) * CHUNK]
+                qkv_v[:, pl.ds(j * WIDTH + k * CHUNK, CHUNK)] = value.astype(BF16)
+        save("qkv", qkv_v, s_qkv.at[l], save_sem.at[0])
+
+    pairs = WIDTH // (2 * HEAD_DIM)
+    wide = 2 * HEAD_DIM
+
+    def attend(l, first, last):
+        bias = jnp.where(
+            lax.broadcasted_iota(jnp.int32, (1, SLOTS), 1) < lengths_ref[z], 0.0, MASKED
+        ).astype(F32)
+        lane = lax.broadcasted_iota(jnp.int32, (SLOTS, wide), 1) < HEAD_DIM
+
+        def e_save(p, slot):
+            return (
+                pltpu.make_async_copy(e_v.at[slot], s_expo.at[l, p], e_sem.at[slot, 0]),
+                pltpu.make_async_copy(inv_v.at[slot], s_inv.at[l, p], e_sem.at[slot, 1]),
+            )
+
+        def step(p, carry):
+            slot = lax.rem(p, 2)
+
+            @pl.when(p >= 2)
+            def _():
+                for copy in e_save(p - 2, slot):
+                    copy.wait()
+
+            q = qkv_v[:, pl.ds(pl.multiple_of(p * wide, wide), wide)]
+            k = qkv_v[:, pl.ds(pl.multiple_of(WIDTH + p * wide, wide), wide)]
+            v = qkv_v[:, pl.ds(pl.multiple_of(2 * WIDTH + p * wide, wide), wide)]
+            outs, invs = [], []
+            for h in range(2):
+                mine = jnp.where(lane, q, 0) if h == 0 else jnp.where(lane, 0, q)
+                scores = nt(mine.astype(BF16), k) + bias
+                expo = jnp.exp(scores - jnp.max(scores, -1, keepdims=True))
+                inv = 1.0 / jnp.sum(expo, -1, keepdims=True)
+                expo = expo.astype(BF16)
+                e_v[slot, h] = expo
+                invs.append(inv)
+                outs.append(nn(expo, v) * inv)
+            inv_v[slot] = jnp.where(lane, invs[0], invs[1])
+            mixed = jnp.where(lane, outs[0], outs[1])
+            mixed_v[:, pl.ds(pl.multiple_of(p * wide, wide), wide)] = mixed
+            mix_v[:, pl.ds(pl.multiple_of(p * wide, wide), wide)] = mixed.astype(BF16)
+            for copy in e_save(p, slot):
+                copy.start()
+            return carry
+
+        lax.fori_loop(first, last, step, 0)
+        if last == pairs:
+            for p in (pairs - 2, pairs - 1):
+                for copy in e_save(p, p % 2):
+                    copy.wait()
+
+    def attention_out(l):
+        copy = load(3, g_out.at[l])
+        copy.wait()
+        for k in range(WIDTH // CHUNK):
+            cols = pl.ds(k * CHUNK, CHUNK)
+            acc_v[:, cols] = nn(mix_v[...], weight(3, cols))
+        save("mix", mixed_v, s_mix.at[l], save_sem.at[1])
+        settle("n0")
+        settle("rs0")
+
+        def body(rr, base):
+            total = state_v[rr] + acc_v[rr] + ob_ref[l:l + 1]
+            value = norm_rows(total, gain1_ref[l:l + 1], b1_ref[l:l + 1], rr, 0)
+            normed_v[rr] = value
+            xb_v[rr] = value.astype(BF16)
+        rows_loop(body)
+        save("n0", n_v.at[0], s_n.at[l, 0], save_sem.at[2])
+        save("rs0", rs_v.at[0], s_rs.at[l, 0], save_sem.at[3])
+
+    def feed_up(l, i):
+        block = rank(i)
+        ff_core(l, block).wait_recv()
+        base = 2 * (i % 2)
+        loads = [load(base + j, g_ff.at[l, block, j]) for j in range(2)]
+        loads[0].wait()
+        settle(("gp", i % 2))
+        for k in range(WIDTH // CHUNK):
+            cols = pl.ds(k * CHUNK, CHUNK)
+            shift = hb_ref[l:l + 1, pl.ds(pl.multiple_of(block * WIDTH + k * CHUNK, CHUNK), CHUNK)]
+            hidden = nn(xb_v[...], weight(base, cols)) + shift
+            share = 0.5 + 0.5 * lax.erf(hidden * ROOT_HALF)
+            active_v[:, cols] = (hidden * share).astype(BF16)
+            slope = share + hidden * (jnp.exp(hidden * hidden * -0.5) * ROOT_TAU)
+            gp_v[i % 2, :, cols] = slope.astype(BF16)
+        save(("gp", i % 2), gp_v.at[i % 2], s_gp.at[l, block], gp_sem.at[i % 2])
+        waiting.append(loads[1])
+
+    def feed_down(l, i):
+        base = 2 * (i % 2)
+        waiting.pop().wait()
+        for k in range(2):
+            cols = pl.ds(k * SLOTS, SLOTS)
+            value = nt(active_v[...], weight_rows(base + 1, k))
+            if i == 0:
+                acc_v[:, cols] = value
+            else:
+                acc_v[:, cols] += value
+
+    def finish(l):
+        settle("n1")
+        settle("rs1")
+
+        def body(rr, base):
+            total = normed_v[rr] + acc_v[rr] + db_ref[l:l + 1]
+            value = norm_rows(total, gain2_ref[l:l + 1], b2_ref[l:l + 1], rr, 1)
+            state_v[rr] = value
+            xb_v[rr] = value.astype(BF16)
+        rows_loop(body)
+        save("n1", n_v.at[1], s_n.at[l, 1], save_sem.at[4])
+        save("rs1", rs_v.at[1], s_rs.at[l, 1], save_sem.at[5])
+
+    greet(near_x, near_y, twin, s, z)
+    for l in range(LAYERS):
+        for copy in own[l]:
+            copy.start()
+    tok_copies, tok_own = row_copies(tokens_ref, tok_v, tok_s, tok_r)
+    for copy in tok_copies:
+        go(copy)
+    tok_own.start()
+    at_send(0, 1)
+    for l in range(LAYERS):
+        dn_v[l] = down_ref[l].T
+        own_down[l].start()
+    at_send(0, 0)
+    own[0][2].wait()
+    own_down[0].wait()
+    ff_send(0)
+    ff_spread(0, 0)
+    own[1][2].wait()
+    own_down[1].wait()
+    ff_send(1)
+    own[0][0].wait()
+    at_pass(0, 0, 0)
+    at_pass(0, 0, 1)
+    at_send(1, 0)
+    ff_spread(0, 1)
+    ff_relay(0, 1, 1)
+    ff_spread(1, 0)
+    own[1][0].wait()
+    at_pass(1, 0, 1)
+    at_pass(1, 0, 0)
+    at_share(0, 0)
+    own[0][1].wait()
+    at_pass(0, 1, 0)
+    ff_cross(0, 0, 1)
+    ff_relay(0, 2, 0)
+    ff_relay(1, 1, 0)
+    ff_cross(0, 1, 1)
+    tok_own.wait()
+    for copy in tok_copies:
+        copy.wait_recv()
+    start_state()
+    ff_relay(0, 1, 0)
+    ff_cross(0, 0, 0)
+    at_send(1, 1)
+    ff_relay(0, 2, 1)
+    ff_relay(0, 3, 1)
+    ff_cross(0, 1, 0)
+    at_core(0, 0).wait_recv()
+    project(0)
+    ff_cross(0, 2, 1)
+    attend(0, 0, 2)
+    ff_cross(0, 2, 0)
+    attend(0, 2, 4)
+    at_pass(0, 1, 1)
+    ff_spread(1, 1)
+    attend(0, 4, 6)
+    ff_share(0, 0)
+    at_share(1, 0)
+    ff_cross(0, 3, 1)
+    ff_relay(0, 3, 0)
+    ff_cross(0, 3, 0)
+    at_share(0, 1)
+    attend(0, 6, 8)
+    ff_cross(1, 0, 1)
+    ff_relay(1, 2, 0)
+    ff_share(0, 1)
+    ff_cross(1, 0, 0)
+    at_core(0, 1).wait_recv()
+    attention_out(0)
+    feed_up(0, 0)
+    ff_share(0, 2)
+    feed_down(0, 0)
+    feed_up(0, 1)
+    ff_cross(1, 1, 0)
+    ff_relay(1, 2, 1)
+    own[1][1].wait()
+    at_pass(1, 1, 1)
+    ff_relay(1, 1, 1)
+    ff_share(0, 3)
+    feed_down(0, 1)
+    at_pass(1, 1, 0)
+    feed_up(0, 2)
+    ff_cross(1, 1, 1)
+    feed_down(0, 2)
+    feed_up(0, 3)
+    feed_down(0, 3)
+    finish(0)
+    ff_relay(1, 3, 0)
+    ff_cross(1, 2, 1)
+    ff_cross(1, 2, 0)
+    at_core(1, 0).wait_recv()
+    project(1)
+    ff_share(1, 0)
+    settle("mix")
+    attend(1, 0, 2)
+    at_share(1, 1)
+    attend(1, 2, 4)
+    attend(1, 4, 6)
+    ff_relay(1, 3, 1)
+    ff_cross(1, 3, 0)
+    ff_cross(1, 3, 1)
+    attend(1, 6, 8)
+    ff_share(1, 1)
+    at_core(1, 1).wait_recv()
+    attention_out(1)
+    feed_up(1, 0)
+    ff_share(1, 2)
+    feed_down(1, 0)
+    feed_up(1, 1)
+    cot_copies, cot_own = row_copies(cot_ref, cot_row, cot_s, cot_r)
+    for copy in cot_copies:
+        go(copy)
+    cot_own.start()
+    ff_share(1, 3)
+    feed_down(1, 1)
+    feed_up(1, 2)
+    feed_down(1, 2)
+    feed_up(1, 3)
+    feed_down(1, 3)
+    finish(1)
+    save("act", xb_v, act_row, save_sem.at[6])
+    for key in list(saves):
+        settle(key)
+    cot_own.wait()
+    for copy in cot_copies:
+        copy.wait_recv()
+    for copy in sent:
+        copy.wait_send()
+    for l in range(LAYERS):
+        ff_drain(l)
+
+
+def forward(lengths, separators, tokens, cotangent, project_in, project_out, up, down, small):
+    shape = jax.ShapeDtypeStruct
+    dma = pltpu.SemaphoreType.DMA
+    vmem = lambda *dims_type: pltpu.VMEM(dims_type[:-1], dims_type[-1])
+    L = LAYERS
+    pairs = WIDTH // (2 * HEAD_DIM)
+    out_shape = (
+        shape((L, 2, 2, 2, QUARTER, 3 * WIDTH), BF16),
+        shape((L, 2, 2, 2, QUARTER, WIDTH), BF16),
+        shape((L, RING, 2, 2, 2, 2, QUARTER, WIDTH), BF16),
+        shape((SLOTS, WIDTH), BF16),
+        shape((SLOTS, WIDTH), BF16),
+        shape((L, SLOTS, 3 * WIDTH), BF16),
+        shape((L, SLOTS, WIDTH), F32),
+        shape((L, pairs, 2, SLOTS, SLOTS), BF16),
+        shape((L, pairs, SLOTS, 2 * HEAD_DIM), F32),
+        shape((L, 2, SLOTS, WIDTH), BF16),
+        shape((L, 2, SLOTS, 128), F32),
+        shape((L, RING, SLOTS, WIDTH), BF16),
+    )
+    anywhere = pl.BlockSpec(memory_space=pl.ANY)
+    scalar = pl.BlockSpec(memory_space=pltpu.SMEM)
+    inside = pl.BlockSpec(memory_space=pltpu.VMEM)
+    return pl.pallas_call(
+        forward_kernel,
+        out_shape=out_shape,
+        in_specs=[scalar] * 2 + [anywhere] * 5 + [inside] * (2 + len(small) - 1),
+        out_specs=[anywhere] * len(out_shape),
+        scratch_shapes=[
+            vmem(SLOTS, WIDTH, BF16), vmem(SLOTS, WIDTH, F32), vmem(SLOTS, WIDTH, BF16),
+            vmem(SLOTS, 3 * WIDTH, BF16), vmem(SLOTS, WIDTH, BF16), vmem(SLOTS, WIDTH, F32),
+            vmem(2, SLOTS, WIDTH, BF16), vmem(2, SLOTS, 128, F32), vmem(SLOTS, WIDTH, F32), vmem(SLOTS, WIDTH, F32),
+            vmem(SLOTS, WIDTH, BF16), vmem(2, SLOTS, WIDTH, BF16), vmem(2, 2, SLOTS, SLOTS, BF16),
+            vmem(2, SLOTS, 2 * HEAD_DIM, F32), vmem(4, 2, 2, 2, QUARTER, WIDTH, BF16),
+            vmem(L, QUARTER, WIDTH, BF16),
+            dma((RING,)), dma((RING,)), dma((RING,)), dma((RING,)),
+            dma((L, 2, 5)), dma((L, 2, 5)), dma((L, 2)), dma((L, 2)),
+            dma((L, RING, 2, 2)), dma((L, RING, 2)), dma((L, RING, 2)), dma((L, RING, 2)),
+            dma((L, RING)), dma((L, RING)),
+            dma((L, 3)), dma((L,)), dma((4,)), dma((7,)), dma((2, 2)), dma((2,)),
+        ],
+        compiler_params=pltpu.CompilerParams(
+            collective_id=0, has_side_effects=True, vmem_limit_bytes=56 << 20
+        ),
+        cost_estimate=pl.CostEstimate(flops=30 * 10**9, bytes_accessed=150 << 20, transcendentals=10**7),
+    )(lengths, separators, tokens, cotangent, project_in, project_out, up, down, *small)
+
+
+TOTAL_ROWS = 32
+
+
+def sum_row(l, kind):
+    if l == 0:
+        return kind if kind < 2 else 6 + kind
+    return 16 + kind
+
+
+def backward_kernel(
+    gain1_ref, gain2_ref,
+    w_in, w_out, w_ff, cot_row, act_row, s_qkv, s_mix, s_expo, s_inv, s_n, s_rs, s_gp,
+    act_out, grad_out, sums_out,
+    g_v, gs_v, acc_v, low_v, gh_v, gm_v, gp_v, gproj_v, out_v, n_v, rs_v, slope_v, qkv_v, mix_v, e_v, inv_v,
+    ff_v, wout_v, win_v, part_v, sum_v, got_v, gotz_v,
+    a_s, a_r, o_s, o_r, r_s, r_r, z_s, z_r,
+    ff_sem, w_sem, n_sem, slope_sem, e_sem, row_sem, own_sem,
+):
+    s, z, c, x, y = place()
+    near_x, near_y, twin = peers(s, z, c, x, y)
+    wide = 2 * HEAD_DIM
+    pairs = WIDTH // wide
+    sent = []
+
+    def remote(src, dst, ss, rs, device):
+        return pltpu.make_async_remote_copy(
+            src_ref=src, dst_ref=dst, send_sem=ss, recv_sem=rs, device_id=device, device_id_type=MESH
+        )
+
+    def go(copy):
+        copy.start()
+        sent.append(copy)
+
+    def fetch(src, dst, sem):
+        return pltpu.make_async_copy(src, dst, sem)
+
+    layers = list(reversed(range(LAYERS)))
+
+    def norm_loads(l):
+        return [fetch(s_n.at[l, k], n_v.at[k], n_sem.at[k]) for k in range(2)] + [
+            fetch(s_rs.at[l, k], rs_v.at[k], n_sem.at[2 + k]) for k in range(2)
+        ]
+
+    def block_loads(l, i):
+        slot = i % 2
+        return [
+            fetch(w_ff.at[l, i, 1], ff_v.at[slot, 1], ff_sem.at[slot, 1]),
+            fetch(s_gp.at[l, i], slope_v.at[slot], slope_sem.at[slot]),
+            fetch(w_ff.at[l, i, 0], ff_v.at[slot, 0], ff_sem.at[slot, 0]),
+        ]
+
+    def out_load(l):
+        return fetch(w_out.at[l], wout_v, w_sem.at[0])
+
+    def in_load(l):
+        return fetch(w_in.at[l], win_v, w_sem.at[1])
+
+    def row_loads(l):
+        return [fetch(s_qkv.at[l], qkv_v, row_sem.at[0]), fetch(s_mix.at[l], mix_v, row_sem.at[1])]
+
+    depth = 4
+
+    def expo_loads(step):
+        l, p, slot = LAYERS - 1 - lax.div(step, pairs), lax.rem(step, pairs), lax.rem(step, depth)
+        return (
+            fetch(s_expo.at[l, p], e_v.at[slot], e_sem.at[slot, 0]),
+            fetch(s_inv.at[l, p], inv_v.at[slot], e_sem.at[slot, 1]),
+        )
+
+    def start(copies):
+        for copy in copies:
+            copy.start()
+
+    def wait(copies):
+        for copy in copies:
+            copy.wait()
+
+    def reduce_stage(which, first, rows, stage):
+        here = pl.ds(first, rows)
+        if stage > 0 and stage < 4:
+            remote(sum_v.at[stage - 1, here], got_v.at[which, stage - 1, here], r_s.at[which, stage - 1],
+                   r_r.at[which, stage - 1], twin).wait_recv()
+            sum_v[stage, here] = sum_v[stage - 1, here] + got_v[which, stage - 1, here]
+        if stage < 3:
+            go(remote(sum_v.at[stage, here], got_v.at[which, stage, here], r_s.at[which, stage],
+                      r_r.at[which, stage], (twin, near_x, near_y)[stage]))
+        elif stage == 3:
+            gotz_v[which, z, here] = sum_v[3, here]
+            for step in range(1, RING):
+                to = lax.rem(z + step, RING)
+                go(remote(sum_v.at[3, here], gotz_v.at[which, z, here], z_s.at[which, step], z_r.at[which, step],
+                          (s, to)))
+        else:
+            for step in range(1, RING):
+                to = lax.rem(z + step, RING)
+                remote(sum_v.at[3, here], gotz_v.at[which, z, here], z_s.at[which, step], z_r.at[which, step],
+                       (s, to)).wait_recv()
+            total = gotz_v[which, 0, here]
+            for k in range(1, RING):
+                total = total + gotz_v[which, k, here]
+            sums_out[here] = total
+
+    def fold(value):
+        total = value[0:8]
+        for k in range(1, value.shape[0] // 8):
+            total = total + value[8 * k:8 * k + 8]
+        return total
+
+    def rows_loop(body, rows=64):
+        def step(r, carry):
+            body(pl.ds(pl.multiple_of(r * rows, rows), rows))
+            return carry
+        lax.fori_loop(0, SLOTS // rows, step, 0)
+
+    def put(at, value):
+        sum_v[0, pl.ds(at, 1)] = value
+
+    def norm_back(grad, gain, which, rr):
+        n = n_v[which, rr].astype(F32)
+        u = grad * gain
+        mean = jnp.sum(u, -1, keepdims=True) * (1.0 / WIDTH)
+        tilt = jnp.sum(u * n, -1, keepdims=True) * (1.0 / WIDTH)
+        return (u - mean - n * tilt) * rs_v[which, rr, 0:1]
+
+    def layer_back(l, last):
+        row = functools.partial(sum_row, l)
+        wait(norm_loads(l)[1::2])
+        part_v[...] = jnp.zeros_like(part_v)
+
+        def second(rr):
+            grad = g_v[rr]
+            part_v[0] += fold(grad)
+            out = norm_back(grad, gain2_ref[l:l + 1], 1, rr)
+            part_v[1] += fold(out)
+            gs_v[rr] = out
+            low_v[rr] = out.astype(BF16)
+        rows_loop(second)
+        put(row(5), jnp.sum(part_v[0], 0, keepdims=True))
+        put(row(4), jnp.sum(part_v[1], 0, keepdims=True))
+
+        for i in range(RING):
+            slot = i % 2
+            loads = block_loads(l, i)
+            wait(loads[:2])
+            for k in range(WIDTH // CHUNK):
+                cols = pl.ds(k * CHUNK, CHUNK)
+                value = nn(low_v[...], ff_v[slot, 1, :, cols]) * slope_v[slot, :, cols].astype(F32)
+                sum_v[0, pl.ds(row(6 + i), 1), cols] = jnp.sum(value, 0, keepdims=True)
+                gh_v[:, cols] = value.astype(BF16)
+            loads[2].wait()
+            for k in range(2):
+                cols = pl.ds(k * SLOTS, SLOTS)
+                value = nt(gh_v[...], ff_v[slot, 0, pl.ds(k * SLOTS, SLOTS)])
+                if i == 0:
+                    acc_v[:, cols] = value
+                else:
+                    acc_v[:, cols] += value
+            if i + 2 < RING:
+                start(block_loads(l, i + 2))
+            elif not last:
+                start(block_loads(l - 1, i - 2))
+
+        wait(norm_loads(l)[0::2])
+        part_v[...] = jnp.zeros_like(part_v)
+
+        def first(rr):
+            grad = gs_v[rr] + acc_v[rr]
+            part_v[0] += fold(grad)
+            out = norm_back(grad, gain1_ref[l:l + 1], 0, rr)
+            part_v[1] += fold(out)
+            gs_v[rr] = out
+            low_v[rr] = out.astype(BF16)
+        rows_loop(first)
+        put(row(3), jnp.sum(part_v[0], 0, keepdims=True))
+        put(row(2), jnp.sum(part_v[1], 0, keepdims=True))
+        if not last:
+            start(norm_loads(l - 1))
+
+        out_load(l).wait()
+        for k in range(2):
+            gm_v[:, pl.ds(k * SLOTS, SLOTS)] = nt(low_v[...], wout_v[pl.ds(k * SLOTS, SLOTS)]).astype(BF16)
+        if not last:
+            out_load(l - 1).start()
+
+        wait(row_loads(l))
+        lane = lax.broadcasted_iota(jnp.int32, (SLOTS, wide), 1) < HEAD_DIM
+        offset = layers.index(l) * pairs
+
+        def attend(p, carry):
+            step = offset + p
+            slot = lax.rem(step, depth)
+            for copy in expo_loads(step):
+                copy.wait()
+            at = lambda k: pl.ds(pl.multiple_of(k * WIDTH + p * wide, wide), wide)
+            q, k, v = qkv_v[:, at(0)], qkv_v[:, at(1)], qkv_v[:, at(2)]
+            gm = gm_v[:, at(0)].astype(F32) * inv_v[slot]
+            mixed = mix_v[:, at(0)]
+            gq, gk, gv = [], [], []
+            for h in range(2):
+                mine = lane if h == 0 else jnp.logical_not(lane)
+                low = jnp.where(mine, gm, 0.0).astype(BF16)
+                inner = jnp.sum(low.astype(F32) * mixed, -1, keepdims=True)
+                expo = e_v[slot, h]
+                gs = (expo.astype(F32) * (nt(low, v) - inner)).astype(BF16)
+                gq.append(nn(gs, k))
+                gk.append(tn(gs, q))
+                gv.append(tn(expo, low))
+            gq = (jnp.where(lane, gq[0], gq[1]) * (HEAD_DIM ** -0.5)).astype(BF16)
+            gv = (gv[0] + gv[1]).astype(BF16)
+            gproj_v[:, at(0)] = gq
+            gproj_v[:, at(1)] = jnp.where(lane, gk[0], gk[1]).astype(BF16)
+            gproj_v[:, at(2)] = gv
+            sum_v[0, pl.ds(row(0), 1), at(0)] = jnp.sum(gq.astype(F32), 0, keepdims=True)
+            sum_v[0, pl.ds(row(1), 1), at(0)] = jnp.sum(gv.astype(F32), 0, keepdims=True)
+
+            @pl.when(step + depth < LAYERS * pairs)
+            def _():
+                for copy in expo_loads(step + depth):
+                    copy.start()
+            return carry
+
+        if not last:
+            lax.fori_loop(0, pairs, attend, 0)
+            start(row_loads(l - 1))
+            in_load(l).wait()
+            for k in range(WIDTH // CHUNK):
+                cols = pl.ds(k * CHUNK, CHUNK)
+                g_v[:, cols] = gs_v[:, cols] + nt(gproj_v[...], win_v[pl.ds(k * CHUNK, CHUNK)])
+            in_load(l - 1).start()
+        else:
+            reduce_stage(0, 8, TOTAL_ROWS - 8, 0)
+            for stage in range(1, 5):
+                lax.fori_loop((stage - 1) * 2, stage * 2, attend, 0)
+                reduce_stage(0, 8, TOTAL_ROWS - 8, stage)
+            reduce_stage(1, 0, 8, 0)
+            in_load(l).wait()
+            for k in range(WIDTH // CHUNK):
+                cols = pl.ds(k * CHUNK, CHUNK)
+                out_v[:, cols] = (gs_v[:, cols] + nt(gproj_v[...], win_v[pl.ds(k * CHUNK, CHUNK)])).astype(BF16)
+                for step in range(1, RING):
+                    go(grad_copy(step, k))
+                grad_own(k).start()
+                if k > 0:
+                    reduce_stage(1, 0, 8, k)
+
+    def part(to):
+        return pl.ds(pl.multiple_of(to * QUARTER, QUARTER), QUARTER)
+
+    def act_copy(step):
+        to = lax.rem(z + step, RING)
+        return remote(act_row.at[part(to)], act_out.at[z], a_s.at[step], a_r.at[step], (s, to))
+
+    def act_own():
+        return fetch(act_row.at[part(z)], act_out.at[z], own_sem.at[0])
+
+    def grad_copy(step, k):
+        to, cols = lax.rem(z + step, RING), pl.ds(k * CHUNK, CHUNK)
+        return remote(out_v.at[part(to), cols], grad_out.at[z, :, cols], o_s.at[step, k], o_r.at[step, k], (s, to))
+
+    def grad_own(k):
+        cols = pl.ds(k * CHUNK, CHUNK)
+        return fetch(out_v.at[part(z), cols], grad_out.at[z, :, cols], own_sem.at[1 + k])
+
+    top = LAYERS - 1
+    cot = fetch(cot_row, out_v, row_sem.at[2])
+    cot.start()
+    start(norm_loads(top)[1::2])
+    start(block_loads(top, 0))
+    start(block_loads(top, 1))
+    start(norm_loads(top)[0::2])
+    out_load(top).start()
+    start(row_loads(top))
+    for step in range(depth):
+        start(expo_loads(jnp.int32(step)))
+    in_load(top).start()
+    greet(near_x, near_y, twin, s, z)
+    for step in range(1, RING):
+        go(act_copy(step))
+    act_own().start()
+    sum_v[0] = jnp.zeros((TOTAL_ROWS, WIDTH), F32)
+    cot.wait()
+
+    def widen(rr):
+        g_v[rr] = out_v[rr].astype(F32)
+    rows_loop(widen)
+    for l in layers:
+        layer_back(l, l == 0)
+    reduce_stage(1, 0, 8, 4)
+    act_own().wait()
+    for step in range(1, RING):
+        act_copy(step).wait_recv()
+    for k in range(WIDTH // CHUNK):
+        grad_own(k).wait()
+        for step in range(1, RING):
+            grad_copy(step, k).wait_recv()
+    for copy in sent:
+        copy.wait_send()
+
+
+def backward(gains, weights, saved, cot_row, act_row):
+    shape = jax.ShapeDtypeStruct
+    dma = pltpu.SemaphoreType.DMA
+    vmem = lambda *dims_type: pltpu.VMEM(dims_type[:-1], dims_type[-1])
+    rows = TOTAL_ROWS
+    chunks = WIDTH // CHUNK
+    anywhere = pl.BlockSpec(memory_space=pl.ANY)
+    inside = pl.BlockSpec(memory_space=pltpu.VMEM)
+    return pl.pallas_call(
+        backward_kernel,
+        out_shape=(
+            shape((RING, QUARTER, WIDTH), BF16), shape((RING, QUARTER, WIDTH), BF16), shape((rows, WIDTH), F32),
+        ),
+        in_specs=[inside] * 2 + [anywhere] * 12,
+        out_specs=[anywhere, anywhere, inside],
+        scratch_shapes=[
+            vmem(SLOTS, WIDTH, F32), vmem(SLOTS, WIDTH, F32), vmem(SLOTS, WIDTH, F32),
+            vmem(SLOTS, WIDTH, BF16), vmem(SLOTS, WIDTH, BF16), vmem(SLOTS, WIDTH, BF16), vmem(8, 128, BF16),
+            vmem(SLOTS, 3 * WIDTH, BF16), vmem(SLOTS, WIDTH, BF16),
+            vmem(2, SLOTS, WIDTH, BF16), vmem(2, SLOTS, 128, F32), vmem(2, SLOTS, WIDTH, BF16),
+            vmem(SLOTS, 3 * WIDTH, BF16), vmem(SLOTS, WIDTH, F32),
+            vmem(4, 2, SLOTS, SLOTS, BF16), vmem(4, SLOTS, 128, F32),
+            vmem(2, 2, WIDTH, WIDTH, BF16), vmem(WIDTH, WIDTH, BF16), vmem(WIDTH, 3 * WIDTH, BF16),
+            vmem(2, 8, WIDTH, F32), vmem(4, rows, WIDTH, F32), vmem(2, 3, rows, WIDTH, F32),
+            vmem(2, RING, rows, WIDTH, F32),
+            dma((RING,)), dma((RING,)), dma((RING, chunks)), dma((RING, chunks)),
+            dma((2, 3)), dma((2, 3)), dma((2, RING)), dma((2, RING)),
+            dma((2, 2)), dma((2,)), dma((4,)), dma((2,)), dma((4, 2)), dma((3,)), dma((1 + chunks,)),
+        ],
+        compiler_params=pltpu.CompilerParams(
+            collective_id=1, has_side_effects=True, vmem_limit_bytes=60 << 20
+        ),
+        cost_estimate=pl.CostEstimate(flops=40 * 10**9, bytes_accessed=100 << 20, transcendentals=10**6),
+    )(*gains, *weights, cot_row, act_row, *saved)
+
+
+def whole_rows(
+    tokens, lengths, separators, type_table, project_in, project_out, up_weight, down_weight, first_norm_gain,
+    second_norm_gain, query_bias, value_bias, output_bias, first_norm_bias, hidden_bias, down_bias,
+    second_norm_bias, cotangent,
+):
+    small = (
+        type_table, first_norm_gain, second_norm_gain, query_bias, value_bias, output_bias, first_norm_bias,
+        hidden_bias, down_bias, second_norm_bias,
+    )
+    g_in, g_out, g_ff, cot_row, act_row, *saved = forward(
+        lengths, separators, tokens, cotangent, project_in, project_out, up_weight, down_weight, small
+    )
+    weights = (
+        g_in.reshape(LAYERS, WIDTH, 3 * WIDTH),
+        g_out.reshape(LAYERS, WIDTH, WIDTH),
+        g_ff.reshape(LAYERS, RING, 2, WIDTH, WIDTH),
+    )
+    activations, grad, sums = backward((first_norm_gain, second_norm_gain), weights, saved, cot_row, act_row)
+
+    def pick(kind, count=1):
+        return jnp.stack([sums[sum_row(l, kind):sum_row(l, kind) + count].reshape(-1) for l in range(LAYERS)])
+
+    return (
+        activations, grad.astype(F32), pick(0), pick(1), pick(2), pick(3), pick(6, RING), pick(4), pick(5),
+    )
 
 
 def layer_norm(total, gain, bias):
@@ -89,7 +995,7 @@
     return jnp.dot(active, down_part, preferred_element_type=jnp.float32)
 
 
-def local(
+def split_heads_plan(
     tokens,
     lengths,
     separators,
@@ -185,7 +1091,7 @@
         inner_in, inner_out, up_part, down_part = weights
         second_grads[layer] = jnp.sum(grad, 0)
         _, norm_back = jax.vjp(
-            partial(layer_norm, gain=second_norm_gain[layer], bias=second_norm_bias[layer]),
+            functools.partial(layer_norm, gain=second_norm_gain[layer], bias=second_norm_bias[layer]),
             second_sum,
         )
         grad_second = norm_back(grad)[0]
@@ -210,7 +1116,7 @@
         ).astype(jnp.float32)
         first_grads[layer] = jnp.sum(grad_normed, 0)
         _, norm_back = jax.vjp(
-            partial(layer_norm, gain=first_norm_gain[layer], bias=first_norm_bias[layer]), first_sum
+            functools.partial(layer_norm, gain=first_norm_gain[layer], bias=first_norm_bias[layer]), first_sum
         )
         grad_first = norm_back(grad_normed)[0]
         output_grads[layer] = jnp.sum(grad_first, 0)
@@ -276,8 +1182,10 @@
         P(),
         P("seq", "head", None),
     )
+    shape = dict(mesh.shape)
+    fits = shape == {"seq": 8, "head": RING}
     return jax.shard_map(
-        local,
+        whole_rows if fits else split_heads_plan,
         mesh=mesh,
         in_specs=placed,
         out_specs=(

time: 1700 us -> 388 us (0.23)
  waiting for transfers between devices: 1080 us -> 0 us
  Pallas kernels: 0 us -> 372 us
  matrix products: 211 us -> 0 us
  local copies, waits for them, and re-layouts: 164 us -> 3.1 us
  blocking collectives: 133 us -> 0 us
  other arithmetic: 60.7 us -> 5.3 us
  starting transfers between devices: 23.8 us -> 0 us
    all_gather x12 -> x0, waiting for transfers between devices: 409 us -> none  [the longest x2 161 us: local(): lax.all_gather(grad_low[None], 'head', axis=0, tiled=True)]
    pallas_call x0 -> x2, Pallas kernels: none -> 372 us  [the longest x1 273 us: forward(): pl.pallas_call(forward_kernel, out_shape=out_shape, in_specs=[scalar] * 2...]
    reduce_scatter x4 -> x0, waiting for transfers between devices: 302 us -> none  [the longest x2 151 us: local(): lax.psum_scatter(feed_forward(rows_all, up_part, down_part, bias_part).as...]
    all_to_all x5 -> x0, waiting for transfers between devices: 249 us -> none  [the longest x2 137 us: local(): lax.all_to_all(projected.reshape(row_count, slot_part, 3, width), 'head',...]
    dot_general x72 -> x0, matrix products: 211 us -> none  [the longest x8 58.4 us: contract_last(): lax.dot_general(left, right, (((1,), (1,)), ((), ())), preferred_element_...]
    all_to_all x3 -> x0, blocking collectives: 133 us -> none  [the longest x1 74 us: local(): lax.all_to_all(grad_projected, 'head', split_axis=1, concat_axis=3, tiled...]
    psum x1 -> x0, waiting for transfers between devices: 116 us -> none  [local(): lax.psum((jnp.stack(query_grads), jnp.stack(value_grads), jnp.stack(outpu...]
    reshape x8 -> x0, local copies, waits for them, and re-layouts: 41.1 us -> none  [the longest x4 27 us: local(): projected.reshape(row_count, slot_part, 3, width)]
  transfers between devices with their start and end apart: 22 -> 0, of which waited for: 18 -> 0; matrix products, arithmetic and copies ran while one was open for 10% -> 0% of each run, Pallas kernels for 0% -> 0%
where the time goes in v1:
time: 388 us; the launch traced here: 382 us
  Pallas kernels  372 us (96%)
  other arithmetic  5.3 us (1%)
    pallas_call x1, Pallas kernels, forward(): pl.pallas_call(forward_kernel, out_shape=out_shape, in_specs=[scalar] * 2...  273 us
    pallas_call x1, Pallas kernels, backward(): pl.pallas_call(backward_kernel, out_shape=(shape((RING, QUARTER, WIDTH),...  99.4 us

profile of v1, /device:TPU:0, one launch (start us, length us, event | category | flops | bytes accessed | tf_op | source)
XLA Modules:
  0.0 381.5 jit_solution(1605333359849366565)
XLA Ops:
  0.6 272.6 %shard_map.241 = (bf16[2,2,2,2,128,3072]{5,4,3,2,1,0:T(8,128)(2,1)}, bf16[2,2,2,2,128,1024]{5,4,3,2,1,0:T(8,128)(2,1)}, bf16[2,4,2,2,2,2,128,1024]{7,6,5,4,3,2,1...) custom-call(s32[4]{0:T(128)} %lengths_ref.1, ...), custom_call_target="tpu_custom_call" | custom-call | flops 30000001024 | bytes 157286400 | tf_op jit(solution)/shard_map/pallas_call | solution.py:535
  273.3 99.4 %shard_map.242 = (bf16[4,128,1024]{2,1,0:T(8,128)(2,1)}, bf16[4,128,1024]{2,1,0:T(8,128)(2,1)}, f32[32,1024]{1,0:T(8,128)}) custom-call(f32[2,1024]{1,0:T(2,128)} %gain1_ref.3, f32[2,1024]{1,0:T(2,128)} %gain2_ref.3, bf16[2,1024,3072]{2,1,0:T(8,128)(2,1)} %bitcast.14, bf16[2,1024,1024]{2,1,0:T(8,128)(2,1)} %bitcast.15, ...), custom_call_target="tpu_custom_call" | custom-call | flops 40000000000 | bytes 104857600 | tf_op jit(solution)/shard_map/pallas_call | solution.py:867
  372.7 0.0 copy-start
  372.7 1.0 slice_bitcast_fusion.1
  373.6 1.1 fusion
  374.8 0.6 pad_maximum_fusion.5
  375.4 0.6 pad_maximum_fusion
  376.1 0.6 pad_maximum_fusion.3
  376.7 0.6 pad_maximum_fusion.1
  377.3 2.8 convert_element_type.3
  380.1 0.0 copy-done
  380.1 1.0 copy.30
  (2 shorter events, 0.0 us)
Async XLA Ops:
  372.7 7.4 %copy-start = (bf16[4,128,1024]{2,1,0:T(8,128)(2,1)S(1)}, bf16[4,128,1024]{2,1,0:T(8,128)(2,1)}, u32[]{:S(2)}) copy-start(bf16[4,128,1024]{2,1,0:T(8,128)(2,1)} %get-tuple-element.68) | copy-start | bytes 3145732
